TPU v7x, 32 devices: a whole 2x2x4 slice. The times are simulated.
32 devices in a mesh: grp: 2 (over y), dp: 4 (over z), sub: 2 (over x), rep: 2 (over core).
Axes of the slice: x: 2, y: 2, z: 4, core: 2. Of those that a mesh axis runs over, the one named last changes fastest.
Arguments:
- fine: bfloat16 [16, 32, 16, 16, 128], P(('grp', 'dp', 'rep'), 'sub'), parts along dimension 0, may hold values from -6 to 6
- conv_weight: bfloat16 [27, 128, 128], replicated, may hold values from -0.109375 to 0.109375
- query_weight: bfloat16 [128, 512], replicated, may hold values from -0.5 to 0.5
- out_weight: bfloat16 [512, 128], replicated, may hold values from -0.25 to 0.25
- coarse_kv: bfloat16 [8, 64, 2, 8, 512], P(('grp', 'sub', 'rep'), 'dp'), parts along dimension 0, may hold values from -6 to 6
- key_bias: bfloat16 [8, 64, 8], P(('grp', 'sub', 'rep'), 'dp'), parts along dimension 0, may hold values from -2 to 303
- zone_ids: int32 [16, 2, 16], P(('grp', 'dp', 'rep'), 'sub'), parts along dimension 0, may hold values from 0 to 63, as said below
- zone_counts: int32 [16, 2], P(('grp', 'dp', 'rep'), 'sub'), parts along dimension 0, may hold values from 8 to 16
- grad_out: bfloat16 [16, 16, 8, 8, 128], P(('grp', 'dp', 'rep'), 'sub'), parts along dimension 0, may hold values from -6 to 6
Outputs:
- weight_grads: float32 [1146880], P(('grp', 'dp', 'sub', 'rep')), parts along dimension 0
- coarse_grad: float32 [8, 64, 2, 8, 512], P(('grp', 'sub', 'rep'), 'dp'), parts along dimension 0
There are 2 independent parts, one for each index of `grp`. A program takes and returns all parts, laid end to end along the dimension named above; an argument that names none is the same for every part. Nothing has to cross between parts.
Inputs may be any that keep to these rules, and one draw needn't show every extreme that they name: `zone_ids`: among all 16 entries of the lists of the 1 patches at positions s .. s + 1 - 1 of one track (used or not), at most 8 entries lie in one block of 16 consecutive tile numbers; in every lane one block is named exactly 8 times by each such group of patches of that lane.
All inputs are finite; a program needn't handle non-finite values.
Results may differ from a plain program's by a relative error of at most 0.0058.
Values may be sent and summed in bfloat16 or wider, within the bound.
A program may use at most 64 MiB of HBM per device.

v0:
```python
import jax
import jax.numpy as jnp
from jax import lax
from jax.sharding import PartitionSpec as P

HEADS = 8


def from_behind(block, axis, distance):
    devices = range(lax.axis_size(axis))
    route = [(i - distance, i) for i in devices if i - distance in devices]
    return lax.ppermute(block, axis, route)


def silu_grad(value):
    sig = jax.nn.sigmoid(value)
    return sig * (1.0 + value * (1.0 - sig))


def conv_operands(strip_cells, lower_plane):
    strip_len = strip_cells.shape[0]
    side_len = strip_cells.shape[1]
    channels = strip_cells.shape[3]
    out_x = strip_len // 2
    out_y = side_len // 2
    out_z = side_len // 2
    parity = strip_cells.reshape(out_x, 2, out_y, 2, out_z, 2 * channels)
    before = lower_plane.reshape(1, out_y, 2, out_z, 2 * channels)
    along_x = [jnp.concatenate([before, parity[:-1, 1]], axis=0), parity[:, 0], parity[:, 1]]
    zero_y = jnp.zeros((out_x, 1, out_z, 2 * channels), strip_cells.dtype)
    zero_z = jnp.zeros((out_x, out_y, 1, channels), strip_cells.dtype)
    operands = []
    for plane_x in along_x:
        along_y = [
            jnp.concatenate([zero_y, plane_x[:, :-1, 1]], axis=1),
            plane_x[:, :, 0],
            plane_x[:, :, 1],
        ]
        for plane_y in along_y:
            both_z = plane_y.reshape(-1, 2 * channels)
            prev_z = jnp.concatenate([zero_z, plane_y[:, :, :-1, channels:]], axis=2).reshape(
                -1, channels
            )
            operands.append((both_z, prev_z))
    return operands


def per_device(
    fine,
    conv_weight,
    query_weight,
    out_weight,
    coarse_kv,
    key_bias,
    zone_ids,
    zone_counts,
    grad_out,
):
    strip_cells = fine[0]
    strip_len = strip_cells.shape[0]
    channels = strip_cells.shape[3]
    lower_plane = from_behind(strip_cells[strip_len - 1 :], "sub", 1)
    operands = conv_operands(strip_cells, lower_plane)
    row_count = operands[0][0].shape[0]
    pre_act = jnp.zeros((row_count, channels), jnp.float32)
    for pair_index in range(9):
        both_z, prev_z = operands[pair_index]
        base = pair_index * 3
        pair_weight = conv_weight[base + 1 : base + 3].reshape(2 * channels, channels)
        pre_act = pre_act + jnp.dot(both_z, pair_weight, preferred_element_type=jnp.float32)
        pre_act = pre_act + jnp.dot(prev_z, conv_weight[base], preferred_element_type=jnp.float32)
    features = jax.nn.silu(pre_act).astype(jnp.bfloat16)
    patches = zone_ids.shape[1]
    list_len = zone_ids.shape[2]
    tiles_here = coarse_kv.shape[1]
    tile_keys = coarse_kv.shape[3]
    inner = coarse_kv.shape[4]
    head_count = HEADS
    head_size = inner // head_count
    patch_rows = row_count // patches
    ids_flat = zone_ids[0].reshape(-1)
    slot_count = ids_flat.shape[0]
    dp_size = lax.axis_size("dp")
    capacity = 2 * slot_count // dp_size
    owners = ids_flat // tiles_here
    local_idx = ids_flat % tiles_here
    slot_range = jnp.arange(slot_count, dtype=jnp.int32)
    same_owner = owners[:, None] == owners[None, :]
    earlier = slot_range[None, :] < slot_range[:, None]
    ranks = jnp.sum(jnp.where(same_owner & earlier, 1, 0), axis=1).astype(jnp.int32)
    slot_dest = owners * capacity + ranks
    placing = slot_dest[:, None] == jnp.arange(dp_size * capacity, dtype=jnp.int32)[None, :]
    request = jnp.sum(jnp.where(placing, local_idx[:, None], 0), axis=0).reshape(dp_size, capacity)
    gathered, gathered_bias = (
        lax.all_gather(coarse_kv[0], "dp", axis=0, tiled=True),
        lax.all_gather(key_bias[0], "dp", axis=0, tiled=True),
    )
    kv_slots = jnp.take(gathered, ids_flat, axis=0)
    bias_slots = jnp.take(gathered_bias, ids_flat, axis=0)
    asked = lax.all_to_all(request, "dp", split_axis=0, concat_axis=0, tiled=True)
    queries = jnp.dot(features, query_weight, preferred_element_type=jnp.float32).astype(
        jnp.bfloat16
    )
    queries = queries.reshape(patches, patch_rows, head_count, head_size)
    kv_patch = kv_slots.reshape(patches, list_len, 2, tile_keys, inner)
    key_rows = kv_patch[:, :, 0].reshape(patches, list_len * tile_keys, head_count, head_size)
    value_rows = kv_patch[:, :, 1].reshape(patches, list_len * tile_keys, head_count, head_size)
    bias_rows = bias_slots.reshape(patches, list_len * tile_keys).astype(jnp.float32)
    live_lists = jnp.arange(list_len, dtype=jnp.int32)[None, :] < zone_counts[0][:, None]
    live = jnp.repeat(live_lists, tile_keys, axis=1)
    scores = (
        jnp.einsum("pqhd,pkhd->phqk", queries, key_rows, preferred_element_type=jnp.float32) * 0.125
        + bias_rows[:, None, None, :]
    )
    scores = jnp.where(live[:, None, None, :], scores, -jnp.inf)
    row_max = jnp.max(scores, axis=-1, keepdims=True)
    exps = jnp.exp(scores - row_max)
    attn_prob = exps / jnp.sum(exps, axis=-1, keepdims=True)
    prob_bf = attn_prob.astype(jnp.bfloat16)
    attended = jnp.einsum(
        "phqk,pkhd->pqhd", prob_bf, value_rows, preferred_element_type=jnp.float32
    ).astype(jnp.bfloat16)
    attended = attended.reshape(row_count, inner)
    upstream = grad_out[0].reshape(row_count, channels)
    grad_out_w = jnp.einsum("ri,rc->ic", attended, upstream, preferred_element_type=jnp.float32)
    grad_attended = jnp.dot(upstream, out_weight.T, preferred_element_type=jnp.float32).astype(
        jnp.bfloat16
    )
    grad_attended = grad_attended.reshape(patches, patch_rows, head_count, head_size)
    grad_prob = jnp.einsum(
        "pqhd,pkhd->phqk", grad_attended, value_rows, preferred_element_type=jnp.float32
    )
    grad_values = jnp.einsum(
        "phqk,pqhd->pkhd", prob_bf, grad_attended, preferred_element_type=jnp.float32
    ).astype(jnp.bfloat16)
    row_dot = jnp.sum(attn_prob * grad_prob, axis=-1, keepdims=True)
    grad_scores = (attn_prob * (grad_prob - row_dot)).astype(jnp.bfloat16)
    grad_queries = (
        jnp.einsum("phqk,pkhd->pqhd", grad_scores, key_rows, preferred_element_type=jnp.float32)
        * 0.125
    ).astype(jnp.bfloat16)
    grad_queries = grad_queries.reshape(row_count, inner)
    grad_keys = (
        jnp.einsum("phqk,pqhd->pkhd", grad_scores, queries, preferred_element_type=jnp.float32)
        * 0.125
    ).astype(jnp.bfloat16)
    grad_query_w = jnp.einsum(
        "rc,ri->ci", features, grad_queries, preferred_element_type=jnp.float32
    )
    grad_features = upstream.astype(jnp.float32) + jnp.dot(
        grad_queries, query_weight.T, preferred_element_type=jnp.float32
    )
    grad_slots = jnp.stack(
        [
            grad_keys.reshape(slot_count, tile_keys, inner),
            grad_values.reshape(slot_count, tile_keys, inner),
        ],
        axis=1,
    )
    outgoing = jnp.dot(
        placing.T.astype(jnp.bfloat16),
        grad_slots.reshape(slot_count, -1),
        preferred_element_type=jnp.float32,
    ).astype(jnp.bfloat16)
    outgoing = outgoing.reshape(dp_size, capacity, 2, tile_keys, inner)
    arrived = lax.all_to_all(outgoing, "dp", split_axis=0, concat_axis=0, tiled=True)
    holder_pick = (
        asked.reshape(-1)[:, None] == jnp.arange(tiles_here, dtype=jnp.int32)[None, :]
    ).astype(jnp.bfloat16)
    tile_grad = jnp.dot(
        holder_pick.T, arrived.reshape(dp_size * capacity, -1), preferred_element_type=jnp.float32
    )
    tile_grad = tile_grad.reshape(tiles_here, 2, tile_keys, inner)
    grad_pre = (grad_features * silu_grad(pre_act)).astype(jnp.bfloat16)
    tap_grads = []
    for pair_index in range(9):
        both_z, prev_z = operands[pair_index]
        prev_grad = jnp.einsum("rc,rd->cd", prev_z, grad_pre, preferred_element_type=jnp.float32)
        both_grad = jnp.einsum("rc,rd->cd", both_z, grad_pre, preferred_element_type=jnp.float32)
        tap_grads.append(prev_grad)
        tap_grads.append(both_grad[:channels])
        tap_grads.append(both_grad[channels:])
    grad_conv_w = jnp.stack(tap_grads, axis=0)
    flat_grads = jnp.concatenate(
        [grad_conv_w.reshape(-1), grad_query_w.reshape(-1), grad_out_w.reshape(-1)]
    )
    weight_grads = lax.psum_scatter(
        flat_grads, ("dp", "sub", "rep"), scatter_dimension=0, tiled=True
    )
    return (weight_grads, tile_grad[None])


def solution(mesh):
    in_specs = (
        P(("grp", "dp", "rep"), "sub", None, None, None),
        P(),
        P(),
        P(),
        P(("grp", "sub", "rep"), "dp", None, None, None),
        P(("grp", "sub", "rep"), "dp", None),
        P(("grp", "dp", "rep"), "sub", None),
        P(("grp", "dp", "rep"), "sub"),
        P(("grp", "dp", "rep"), "sub", None, None, None),
    )
    out_specs = (P(("grp", "dp", "sub", "rep")), P(("grp", "sub", "rep"), "dp", None, None, None))
    return jax.shard_map(
        per_device, mesh=mesh, in_specs=in_specs, out_specs=out_specs, check_vma=False
    )
```

profile of v0, /device:TPU:0, one launch (start us, length us, event | category | flops | bytes accessed | tf_op | source)
XLA Modules:
  0.0 216.6 jit_solution(44621596739526856)
XLA Ops:
  7.2 0.7 all-gather.4.cloned.1.call-update
  7.9 0.7 and_select_fusion
  9.5 6.3 %all-to-all-start = ((s32[4,1,8]{2,1,0:T(1,128)}), s32[4,1,8]{2,1,0:T(1,128)S(1)}, u32[]{:S(2)}, u32[]{:S(2)}) async-start(s32[4,1,8]{2,1,0:T(1,128)} %bitcast.101), calls=%async_computation | async-start | bytes 4096 | tf_op jit(solution)/shard_map/all_to_all | solution.py:100
  15.8 0.8 slice_bitcast_fusion.23
  16.7 4.0 %collective-permute-start = (bf16[1,16,16,128]{3,2,1,0:T(8,128)(2,1)S(1)}, bf16[1,16,16,128]{3,2,1,0:T(8,128)(2,1)}, u32[]{:S(2)}, u32[]{:S(2)}) collective-permute-start(bf16[1,16,16,128]{3,2,1,0:T(8,128)(2,1)S(1)} %slice_bitcast_fusion.23), channel_id=1, source_target_pairs={{0,2},{1,3},{4,6},{5,7},{8,10},{9,11},{12,14},{13,15},{16,18},{17,... | collective-permute-start | bytes 196616 | tf_op jit(solution)/shard_map/ppermute | solution.py:12
  21.4 1.2 fusion.70
  22.5 1.4 reshape_squeeze.31
  24.2 1.1 slice_bitcast_fusion.24
  26.2 13.8 %all-gather.1 = bf16[1,64,8]{2,1,0:T(8,128)(2,1)S(1)} all-gather(bf16[1,16,8]{2,1,0:T(8,128)(2,1)S(1)} %copy.63), channel_id=3, replica_groups=mesh['grp'=2,'dp'=4,'sub'=2,'rep'=2] {'dp'}, dimensions={1}, use_global_device_ids=true | all-gather | bytes 1280 | tf_op jit(solution)/shard_map/all_gather | solution.py:96
  41.2 1.9 fusion.73
  43.2 2.1 convolution_convert_fusion.2
  45.7 0.7 concatenate.49
  46.5 0.7 concatenate.50
  47.2 0.9 reshape.344
  49.2 1.0 convolution_add_fusion.17
  50.4 1.0 convolution_add_fusion.15
  51.6 1.0 convolution_add_fusion.13
  52.9 1.0 convolution_add_fusion.11
  54.1 1.0 convolution_add_fusion.9
  55.3 1.0 convolution_add_fusion.7
  56.5 0.9 convolution_add_fusion.5
  57.7 0.9 convolution_add_fusion.3
  58.9 0.9 convolution_add_fusion.1
  59.8 0.7 copy-done.28
  60.5 1.2 convolution_convert_fusion.3
  61.7 1.8 gather_fusion
  63.6 0.7 fusion.74
  64.3 1.1 reshape.346
  65.4 0.8 copy.65
  66.3 1.1 reshape.369
  67.4 0.8 copy.64
  68.2 3.4 %fusion.75 = (f32[8,512]{1,0:T(8,128)S(1)}, f32[8,512,128]{1,2,0:T(8,128)}) fusion(f32[128]{0:T(128)} %reshape.378, pred[128]{0:T(512)(128)(4,1)S(1)} %broadcast_in_dim.75, bf16[512,8,64]{0,2,1:T(8,128)(2,1)} %bitcast.410, bf16[128,8,64]{0,2,1:T(8,128)(2,1)} %copy.65), kind=kOutput, calls=%fused_computation.180 | convolution fusion | flops 69730432 | bytes 2769536 | tf_op jit(solution)/shard_map/sub | solution.py:117
  71.6 3.0 %fusion.6 = bf16[1,128,8,64]{1,3,2,0:T(8,128)(2,1)} fusion(bf16[512,8,64]{0,2,1:T(8,128)(2,1)} %bitcast.408, f32[8,512,128]{1,2,0:T(8,128)} %get-tuple-element.36, f32[8,512]{1,0:T(8,128)S(1)} %get-tuple-element.35), kind=kOutput, calls=%fused_computation.45 | convolution fusion | flops 68222976 | bytes 2768896 | tf_op jit(solution)/shard_map/phqk,pqhd->pkhd/dot_general | solution.py:133
  74.7 1.1 convolution_convert_fusion.1
  77.3 1.1 fusion.7
  79.2 1.0 convolution_bitcast_fusion.2
  80.2 0.9 convolution_bitcast_fusion.3
  81.1 0.9 convolution_bitcast_fusion.4
  82.0 0.9 fusion.81
  82.9 0.9 convolution_bitcast_fusion.5
  83.9 0.9 convolution_bitcast_fusion.6
  84.8 0.9 fusion.80
  85.7 0.9 fusion.79
  86.6 0.9 fusion.78
  87.6 0.9 fusion.77
  88.7 1.1 copy.77
  89.8 0.9 stack_reshape.7
  90.7 1.3 convolution_bitcast_fusion
  92.0 1.8 copy.90
  93.8 1.8 copy.75
  95.6 1.2 stack_reshape.6
  96.8 1.0 pad_maximum_fusion.2
  97.8 0.9 copy.91
  98.7 0.9 fusion.46
  99.5 0.8 fusion.45
  102.6 1.6 pad_maximum_fusion
  104.2 0.9 copy-done.11
  105.1 1.2 convolution_convert_fusion
  106.3 4.4 %all-to-all-start.1 = ((bf16[4,8,2,8,512]{4,1,3,2,0:T(8,128)(2,1)}), bf16[4,8,2,8,512]{4,1,3,2,0:T(8,128)(2,1)S(1)}, u32[]{:S(2)}, u32[]{:S(2)}) async-start(bf16[4,8,2,8,512]{4,1,3,2,0:T(8,128)(2,1)} %bitcast.108), calls=%async_computation.1 | async-start | bytes 1048576 | tf_op jit(solution)/shard_map/all_to_all | solution.py:166
  112.5 0.7 reduce.9
  113.3 15.3 %all-to-all-done.1 = bf16[4,8,2,8,512]{4,1,3,2,0:T(8,128)(2,1)S(1)} async-done(((bf16[4,8,2,8,512]{4,1,3,2,0:T(8,128)(2,1)}), bf16[4,8,2,8,512]{4,1,3,2,0:T(8,128)(2,1)S(1)}, u32[]{:S(2)}, u32[]{:S(2)}) %all-to-all-start.1) | async-done | bytes 524320 | tf_op jit(solution)/shard_map/all_to_all | solution.py:166
  129.2 1.1 copy.80
  130.3 77.9 %all-reduce.15.cloned.1.call-done = f32[573440]{0:T(1024)} async-done(((f32[573440]{0:T(1024)}), f32[573440]{0:T(1024)}) %all-reduce.15.cloned.1.call-update) | async-done | bytes 2293776
  208.2 1.6 dynamic-slice.1
  (174 shorter events, 12.9 us)
Async XLA Ops:
  7.2 53.4 %copy-start = (bf16[128,512]{1,0:T(8,128)(2,1)S(1)}, bf16[128,512]{1,0:T(8,128)(2,1)}, u32[]{:S(2)}) copy-start(bf16[128,512]{1,0:T(8,128)(2,1)} %param.11) | copy-start | bytes 393220
  7.2 54.5 %all-gather.4.cloned.1.call-start = ((), (), s32[]{:S(2)}) async-start(), calls=%async_computation.2 | async-start | bytes 1310720 | tf_op jit(solution)/shard_map/all_gather | solution.py:95
  8.8 12.6 %copy-start.41 = (s32[16]{0:T(128)}, s32[16]{0:T(128)S(1)}, u32[]{:S(2)}) copy-start(s32[16]{0:T(128)S(1)} %multiply_add_fusion) | copy-start | bytes 196
  9.5 96.8 %all-to-all-start = ((s32[4,1,8]{2,1,0:T(1,128)}), s32[4,1,8]{2,1,0:T(1,128)S(1)}, u32[]{:S(2)}, u32[]{:S(2)}) async-start(s32[4,1,8]{2,1,0:T(1,128)} %bitcast.101), calls=%async_computation | async-start | bytes 4096 | tf_op jit(solution)/shard_map/all_to_all | solution.py:100
  15.8 192.4 %all-reduce.15.cloned.1.call-start = ((), (), s32[]{:S(2)}) async-start(), calls=%async_computation.3 | async-start | bytes 4587520
  16.7 30.5 %collective-permute-start = (bf16[1,16,16,128]{3,2,1,0:T(8,128)(2,1)S(1)}, bf16[1,16,16,128]{3,2,1,0:T(8,128)(2,1)}, u32[]{:S(2)}, u32[]{:S(2)}) collective-permute-start(bf16[1,16,16,128]{3,2,1,0:T(8,128)(2,1)S(1)} %slice_bitcast_fusion.23), channel_id=1, source_target_pairs={{0,2},{1,3},{4,6},{5,7},{8,10},{9,11},{12,14},{13,15},{16,18},{17,... | collective-permute-start | bytes 196616 | tf_op jit(solution)/shard_map/ppermute | solution.py:12
  24.1 1.9 copy-start.40
  24.1 2.0 copy-start.39
  43.1 2.4 %copy-start.14 = (bf16[8,8,8,256]{3,2,1,0:T(8,128)(2,1)S(1)}, bf16[8,8,8,256]{3,2,1,0:T(8,128)(2,1)}, u32[]{:S(2)}) copy-start(bf16[8,8,8,256]{3,2,1,0:T(8,128)(2,1)} %get-tuple-element.21) | copy-start | bytes 786436
  43.1 2.5 %copy-start.13 = (bf16[8,8,8,256]{3,2,1,0:T(8,128)(2,1)S(1)}, bf16[8,8,8,256]{3,2,1,0:T(8,128)(2,1)}, u32[]{:S(2)}) copy-start(bf16[8,8,8,256]{3,2,1,0:T(8,128)(2,1)} %get-tuple-element.22) | copy-start | bytes 786436
  43.2 2.5 %copy-start.12 = (bf16[8,8,8,256]{3,2,1,0:T(8,128)(2,1)S(1)}, bf16[8,8,8,256]{3,2,1,0:T(8,128)(2,1)}, u32[]{:S(2)}) copy-start(bf16[8,8,8,256]{3,2,1,0:T(8,128)(2,1)} %get-tuple-element.43) | copy-start | bytes 786436
  48.1 0.8 copy-start.27
  48.2 2.0 copy-start.37
  48.3 3.0 %copy-start.6 = (bf16[8,8,8,128]{3,2,1,0:T(8,128)(2,1)}, bf16[8,8,8,128]{3,2,1,0:T(8,128)(2,1)S(1)}, u32[]{:S(2)}) copy-start(bf16[8,8,8,128]{3,2,1,0:T(8,128)(2,1)S(1)} %concatenate.45) | copy-start | bytes 393220
  48.3 3.0 %copy-start.36 = (bf16[2,128,128]{2,1,0:T(8,128)(2,1)S(1)}, bf16[2,128,128]{2,1,0:T(8,128)(2,1)}, u32[]{:S(2)}) copy-start(bf16[2,128,128]{2,1,0:T(8,128)(2,1)} %get-tuple-element.18) | copy-start | bytes 196612
  48.4 3.2 %copy-start.4 = (bf16[8,8,8,128]{3,2,1,0:T(8,128)(2,1)}, bf16[8,8,8,128]{3,2,1,0:T(8,128)(2,1)S(1)}, u32[]{:S(2)}) copy-start(bf16[8,8,8,128]{3,2,1,0:T(8,128)(2,1)S(1)} %concatenate.46) | copy-start | bytes 393220
  48.5 3.1 %copy-start.8 = (bf16[8,8,8,128]{3,2,1,0:T(8,128)(2,1)}, bf16[8,8,8,128]{3,2,1,0:T(8,128)(2,1)S(1)}, u32[]{:S(2)}) copy-start(bf16[8,8,8,128]{3,2,1,0:T(8,128)(2,1)S(1)} %concatenate.44) | copy-start | bytes 393220
  49.2 3.5 %copy-start.35 = (bf16[2,128,128]{2,1,0:T(8,128)(2,1)S(1)}, bf16[2,128,128]{2,1,0:T(8,128)(2,1)}, u32[]{:S(2)}) copy-start(bf16[2,128,128]{2,1,0:T(8,128)(2,1)} %get-tuple-element.17) | copy-start | bytes 196612
  50.4 3.5 %copy-start.34 = (bf16[2,128,128]{2,1,0:T(8,128)(2,1)S(1)}, bf16[2,128,128]{2,1,0:T(8,128)(2,1)}, u32[]{:S(2)}) copy-start(bf16[2,128,128]{2,1,0:T(8,128)(2,1)} %get-tuple-element.16) | copy-start | bytes 196612
  51.4 2.7 %copy-start.3 = (bf16[8,8,8,128]{3,2,1,0:T(8,128)(2,1)S(1)}, bf16[8,8,8,128]{3,2,1,0:T(8,128)(2,1)}, u32[]{:S(2)}) copy-start(bf16[8,8,8,128]{3,2,1,0:T(8,128)(2,1)} %concatenate.49) | copy-start | bytes 393220
  51.6 3.4 %copy-start.33 = (bf16[2,128,128]{2,1,0:T(8,128)(2,1)S(1)}, bf16[2,128,128]{2,1,0:T(8,128)(2,1)}, u32[]{:S(2)}) copy-start(bf16[2,128,128]{2,1,0:T(8,128)(2,1)} %get-tuple-element.15) | copy-start | bytes 196612
  52.6 2.7 %copy-start.2 = (bf16[8,8,8,128]{3,2,1,0:T(8,128)(2,1)S(1)}, bf16[8,8,8,128]{3,2,1,0:T(8,128)(2,1)}, u32[]{:S(2)}) copy-start(bf16[8,8,8,128]{3,2,1,0:T(8,128)(2,1)} %concatenate.50) | copy-start | bytes 393220
  52.9 3.4 %copy-start.32 = (bf16[2,128,128]{2,1,0:T(8,128)(2,1)S(1)}, bf16[2,128,128]{2,1,0:T(8,128)(2,1)}, u32[]{:S(2)}) copy-start(bf16[2,128,128]{2,1,0:T(8,128)(2,1)} %get-tuple-element.14) | copy-start | bytes 196612
  54.1 3.4 %copy-start.31 = (bf16[2,128,128]{2,1,0:T(8,128)(2,1)S(1)}, bf16[2,128,128]{2,1,0:T(8,128)(2,1)}, u32[]{:S(2)}) copy-start(bf16[2,128,128]{2,1,0:T(8,128)(2,1)} %get-tuple-element.13) | copy-start | bytes 196612
  55.3 3.3 %copy-start.30 = (bf16[2,128,128]{2,1,0:T(8,128)(2,1)S(1)}, bf16[2,128,128]{2,1,0:T(8,128)(2,1)}, u32[]{:S(2)}) copy-start(bf16[2,128,128]{2,1,0:T(8,128)(2,1)} %get-tuple-element.12) | copy-start | bytes 196612
  59.8 0.7 copy-start.28
  71.6 3.0 %copy-start.1 = (f32[8,512,128]{1,2,0:T(8,128)S(1)}, f32[8,512,128]{1,2,0:T(8,128)}, u32[]{:S(2)}) copy-start(f32[8,512,128]{1,2,0:T(8,128)} %get-tuple-element.36) | copy-start | bytes 6291460
  71.6 3.0 %copy-start.38 = (bf16[128,8,64]{0,2,1:T(8,128)(2,1)S(1)}, bf16[128,8,64]{0,2,1:T(8,128)(2,1)}, u32[]{:S(2)}) copy-start(bf16[128,8,64]{0,2,1:T(8,128)(2,1)} %copy.64) | copy-start | bytes 393220
  74.7 1.1 copy-start.15
  76.3 1.0 copy-start.16
  77.3 1.1 copy-start.26
  77.3 1.4 copy-start.17
  77.3 1.4 copy-start.29
  82.0 6.5 %copy-start.9 = (bf16[8,8,8,128]{3,2,1,0:T(8,128)(2,1)S(1)}, bf16[8,8,8,128]{3,2,1,0:T(8,128)(2,1)}, u32[]{:S(2)}) copy-start(bf16[8,8,8,128]{3,2,1,0:T(8,128)(2,1)} %copy-done.8) | copy-start | bytes 393220
  92.0 8.4 %copy-start.7 = (bf16[8,8,8,128]{3,2,1,0:T(8,128)(2,1)S(1)}, bf16[8,8,8,128]{3,2,1,0:T(8,128)(2,1)}, u32[]{:S(2)}) copy-start(bf16[8,8,8,128]{3,2,1,0:T(8,128)(2,1)} %copy-done.6) | copy-start | bytes 393220
  92.0 8.6 %copy-start.5 = (bf16[8,8,8,128]{3,2,1,0:T(8,128)(2,1)S(1)}, bf16[8,8,8,128]{3,2,1,0:T(8,128)(2,1)}, u32[]{:S(2)}) copy-start(bf16[8,8,8,128]{3,2,1,0:T(8,128)(2,1)} %copy-done.4) | copy-start | bytes 393220
  96.7 3.9 %copy-start.25 = (f32[256,128]{1,0:T(8,128)S(1)}, f32[256,128]{1,0:T(8,128)}, u32[]{:S(2)}) copy-start(f32[256,128]{1,0:T(8,128)} %fusion.78) | copy-start | bytes 393220
  96.8 4.2 %copy-start.24 = (f32[256,128]{1,0:T(8,128)S(1)}, f32[256,128]{1,0:T(8,128)}, u32[]{:S(2)}) copy-start(f32[256,128]{1,0:T(8,128)} %fusion.79) | copy-start | bytes 393220
  96.8 4.4 %copy-start.23 = (f32[256,128]{1,0:T(8,128)S(1)}, f32[256,128]{1,0:T(8,128)}, u32[]{:S(2)}) copy-start(f32[256,128]{1,0:T(8,128)} %fusion.80) | copy-start | bytes 393220
  97.8 3.7 %copy-start.22 = (f32[256,128]{1,0:T(8,128)S(1)}, f32[256,128]{1,0:T(8,128)}, u32[]{:S(2)}) copy-start(f32[256,128]{1,0:T(8,128)} %convolution_bitcast_fusion.6) | copy-start | bytes 393220
  97.8 4.0 %copy-start.21 = (f32[256,128]{1,0:T(8,128)S(1)}, f32[256,128]{1,0:T(8,128)}, u32[]{:S(2)}) copy-start(f32[256,128]{1,0:T(8,128)} %convolution_bitcast_fusion.5) | copy-start | bytes 393220
  98.7 3.4 %copy-start.20 = (f32[256,128]{1,0:T(8,128)S(1)}, f32[256,128]{1,0:T(8,128)}, u32[]{:S(2)}) copy-start(f32[256,128]{1,0:T(8,128)} %fusion.81) | copy-start | bytes 393220
  100.6 1.7 copy-start.19
  100.9 1.7 copy-start.18
  101.0 1.7 copy-start.10
  104.2 0.9 copy-start.11
  104.2 1.0 copy-start.42
  104.2 6.6 %copy-start.43 = (u32[32]{0:T(128)S(1)}, u32[32]{0:T(128)}, u32[]{:S(2)}) copy-start(u32[32]{0:T(128)} %constant.106) | copy-start | bytes 388
  106.3 22.3 %all-to-all-start.1 = ((bf16[4,8,2,8,512]{4,1,3,2,0:T(8,128)(2,1)}), bf16[4,8,2,8,512]{4,1,3,2,0:T(8,128)(2,1)S(1)}, u32[]{:S(2)}, u32[]{:S(2)}) async-start(bf16[4,8,2,8,512]{4,1,3,2,0:T(8,128)(2,1)} %bitcast.108), calls=%async_computation.1 | async-start | bytes 1048576 | tf_op jit(solution)/shard_map/all_to_all | solution.py:166
Sparse Core Ops, SparseCore 0:
  9.6 30.8 all-gather.3
  104.3 103.8 all-reduce.14
where the time goes:
time: 218 us; the launch traced here: 217 us
  waiting for transfers between devices  93.9 us (43%)
  matrix products  38 us (17%)
  local copies, waits for them, and re-layouts  32.8 us (15%)
  between operations  16.4 us (8%)
  starting transfers between devices  14.8 us (7%)
  blocking collectives  13.8 us (6%)
  other arithmetic  6.83 us (3%)
    unnamed x3, waiting for transfers between devices  78.6 us
    all_to_all x1, waiting for transfers between devices, per_device(): lax.all_to_all(outgoing, 'dp', split_axis=0, concat_axis=0, tiled=True)  15.3 us
    all_gather x1, blocking collectives, per_device(): lax.all_gather(key_bias[0], 'dp', axis=0, tiled=True)  13.8 us
    unnamed x112, local copies, waits for them, and re-layouts  10.6 us
    dot_general x9, matrix products, per_device(): jnp.dot(prev_z, conv_weight[base], preferred_element_type=jnp.float32)  8.56 us
    dot_general x9, matrix products, per_device(): jnp.einsum('rc,rd->cd', both_z, grad_pre, preferred_element_type=jnp.floa...  8.3 us
    all_to_all x1, starting transfers between devices, per_device(): lax.all_to_all(request, 'dp', split_axis=0, concat_axis=0, tiled=True)  6.32 us
    all_to_all x1, starting transfers between devices, per_device(): lax.all_to_all(outgoing, 'dp', split_axis=0, concat_axis=0, tiled=True)  4.45 us
  transfers between devices with their start and end apart: 5, of which 2 were waited for; matrix products, arithmetic and copies ran while one was open for 34% of the time, Pallas kernels for 0%

commit v1 on v0

v1 whole, which is shorter than its diff:
```python
import functools

import jax
import jax.numpy as jnp
import numpy as np
from jax import lax
from jax.experimental import pallas as pl
from jax.experimental.pallas import tpu as pltpu
from jax.sharding import PartitionSpec as P

HEADS = 8
MESH = pl.DeviceIdType.MESH
F32 = jnp.float32
BF16 = jnp.bfloat16


def dot(a, b):
    return jnp.dot(a, b, preferred_element_type=F32)


def dot_nt(a, b):
    return lax.dot_general(a, b, (((1,), (1,)), ((), ())), preferred_element_type=F32)


def dot_tn(a, b):
    return lax.dot_general(a, b, (((0,), (0,)), ((), ())), preferred_element_type=F32)


def iota(shape, dim):
    return lax.broadcasted_iota(jnp.int32, shape, dim)


def tap_selector(side):
    half = side // 2
    sel = np.zeros((9, half, half, side, side), np.float32)
    for b in range(3):
        for c in range(3):
            for y in range(half):
                for z in range(half):
                    yy, zz = 2 * y + b - 1, 2 * z + c - 1
                    if yy >= 0 and zz >= 0:
                        sel[b * 3 + c, y, z, yy, zz] = 1.0
    return sel.reshape(9 * half * half, side * side)


def kernel(
    cfg,
    fine,
    selector,
    conv_w,
    query_w,
    out_w,
    kv,
    meta,
    upstream,
    weight_out,
    tile_out,
    halo,
    t_even,
    t_odd,
    pre,
    feat,
    query,
    grad_att,
    grad_kv,
    grad_query,
    acc,
    metas,
    kv_send,
    kv_recv,
    slot_send,
    slot_recv,
    picks,
    rep_send,
    rep_recv,
    sub_send,
    sub_recv,
    part,
    dp_send,
    dp_recv,
    halo_sem,
    meta_sem,
    kv_sem,
    slot_sem,
    rep_sem,
    sub_sem,
    dp_sem,
):
    dps, subs, tiles, cap, slots, rows_dev, reduce_here = cfg
    me = lax.axis_index("dp")
    sub = lax.axis_index("sub")
    rep = lax.axis_index("rep")
    cap_rows = cap * 16
    planes = t_even.shape[0]
    cells = t_even.shape[1]
    channels = fine.shape[2]
    lanes = slots * 8
    peers = [lax.rem(me + d, dps) for d in range(dps)]
    behind = [lax.rem(me + dps - d, dps) for d in range(dps)]

    barrier = pltpu.get_barrier_semaphore()
    greeted = 0
    for d in range(1, dps):
        pl.semaphore_signal(barrier, inc=1, device_id={"dp": peers[d]}, device_id_type=MESH)
        greeted += 1
    for step in (1, subs - 1) if subs > 2 else (1,):
        pl.semaphore_signal(
            barrier, inc=1, device_id={"sub": lax.rem(sub + step, subs)}, device_id_type=MESH
        )
        greeted += 1
    pl.semaphore_signal(barrier, inc=1, device_id={"rep": 1 - rep}, device_id_type=MESH)
    greeted += 1
    pl.semaphore_wait(barrier, greeted)

    def send(src, dst, sems, index, where):
        return pltpu.make_async_remote_copy(
            src_ref=src,
            dst_ref=dst,
            send_sem=sems.at[0, index],
            recv_sem=sems.at[1, index],
            device_id=where,
            device_id_type=MESH,
        )

    meta_copies = [
        send(meta, metas.at[me], meta_sem, d, {"dp": peers[d]}) for d in range(1, dps)
    ]
    for copy in meta_copies:
        copy.start()
    halo_copy = send(
        fine.at[2 * planes - 1], halo, halo_sem, 0, {"sub": lax.rem(sub + 1, subs)}
    )
    halo_copy.start()
    metas[me] = meta[...]

    def spread_taps(found, target, index):
        for tap in range(9):
            target[index, :, tap * channels : (tap + 1) * channels] = found[
                tap * cells : (tap + 1) * cells
            ]

    def unfold(i, carry):
        pair = jnp.concatenate([fine[2 * i], fine[2 * i + 1]], axis=1)
        found = dot(selector[...], pair).astype(BF16)
        spread_taps(found[:, :channels], t_even, i)
        spread_taps(found[:, channels:], t_odd, i + 1)
        return carry

    lax.fori_loop(0, planes, unfold, 0)

    for copy in meta_copies:
        copy.wait()

    def slot_dest(ids_row):
        owner_row = jnp.floor(ids_row * (1.0 / tiles))
        owner_col = jnp.transpose(jnp.broadcast_to(owner_row, (lanes, lanes)))
        earlier = (iota((lanes, lanes), 0) // 8) < (iota((lanes, lanes), 1) // 8)
        same = jnp.where((owner_col == owner_row) & earlier, 1.0, 0.0)
        rank = jnp.sum(same, axis=0, keepdims=True) * 0.125
        return owner_row * cap + rank

    me_f = me.astype(F32)

    def picker(ids_row):
        dest = slot_dest(ids_row)
        slot_row = (iota((cap_rows, lanes), 0) // 16).astype(F32) + me_f * cap
        first = (iota((cap_rows, lanes), 1) % 8) == 0
        by_slot = jnp.where((slot_row == dest) & first, 1.0, 0.0).astype(BF16)
        tile_row = (iota((tiles * 16, lanes), 0) // 16).astype(F32) + me_f * tiles
        by_tile = jnp.where(tile_row == ids_row, 1.0, 0.0).astype(BF16)
        matched = dot_nt(by_slot, by_tile)
        unit = (iota(matched.shape, 0) % 16) == (iota(matched.shape, 1) % 16)
        return jnp.where(unit, matched, 0.0).astype(BF16)

    kv_copies = []
    for d in range(dps - 1, -1, -1):
        ids_row = metas[peers[d], tiles : tiles + 1, :]
        pick = picker(ids_row)
        picks[peers[d]] = pick
        chosen = dot(pick, kv[...]).astype(BF16)
        if d == 0:
            kv_recv[me] = chosen
        else:
            kv_send[d - 1] = chosen
            copy = send(kv_send.at[d - 1], kv_recv.at[me], kv_sem, d, {"dp": peers[d]})
            copy.start()
            kv_copies.append(copy)

    halo_copy.wait()
    edge = dot(selector[...], halo[...])
    edge = jnp.where(sub > 0, edge, 0.0).astype(BF16)
    spread_taps(edge, t_odd, 0)

    row_count = planes * cells

    def columns(a):
        if a == 1:
            return t_even[...].reshape(row_count, 9 * channels)
        start = a // 2
        return t_odd[start : start + planes].reshape(row_count, 9 * channels)

    value = dot(columns(0), conv_w[0]) + dot(columns(1), conv_w[1]) + dot(columns(2), conv_w[2])
    pre[...] = value
    feat[...] = (value * jax.nn.sigmoid(value)).astype(BF16)
    query[...] = dot(feat[...], query_w[...]).astype(BF16)
    grad_att[...] = dot_nt(upstream[...], out_w[...]).astype(BF16)

    ids_row = meta[tiles : tiles + 1, :]
    count = meta[tiles + 1 : tiles + 2, :]
    dest = slot_dest(ids_row)
    dest2 = jnp.concatenate([dest, dest], axis=1)
    place_rows = dps * cap_rows
    row_i = iota((place_rows, 2 * lanes), 0)
    lane_i = iota((place_rows, 2 * lanes), 1)
    fits = ((row_i // 16).astype(F32) == dest2) & (
        (row_i % 16) == (lane_i // lanes) * 8 + lane_i % 8
    )
    placing = jnp.where(fits, 1.0, 0.0).astype(BF16)

    bias = jnp.zeros((1, lanes), F32)
    for owner in range(dps):
        tile_row = iota((tiles, lanes), 0).astype(F32) + float(owner * tiles)
        bias = bias + jnp.sum(
            jnp.where(tile_row == ids_row, metas[owner, :tiles, :], 0.0), axis=0, keepdims=True
        )
    lane_slot = (iota((1, lanes), 1) // 8).astype(F32)
    live = lane_slot < count
    bias = jnp.where(live, bias, -jnp.inf)

    for copy in kv_copies:
        copy.wait()
    kv_all = dot_tn(placing, kv_recv[...].reshape(place_rows, kv.shape[1])).astype(BF16)

    low = iota((lanes, 128), 1) < 64
    conv_rows = 27 * channels
    pairs = query.shape[1] // 128
    for j in range(pairs):
        cut = slice(j * 128, (j + 1) * 128)
        keys = kv_all[:lanes, cut]
        values = kv_all[lanes:, cut]
        none = jnp.zeros_like(keys)
        keys2 = jnp.concatenate(
            [jnp.where(low, keys, none), jnp.where(low, none, keys)], axis=0
        )
        values2 = jnp.concatenate(
            [jnp.where(low, values, none), jnp.where(low, none, values)], axis=0
        )
        q = query[:, cut]
        g = grad_att[:, cut]
        scores = dot_nt(q, keys2) * 0.125
        probs = []
        for h in range(2):
            s = scores[:, h * lanes : (h + 1) * lanes] + bias
            e = jnp.exp(s - jnp.max(s, axis=1, keepdims=True))
            probs.append(e / jnp.sum(e, axis=1, keepdims=True))
        prob_b = jnp.concatenate([p.astype(BF16) for p in probs], axis=1)
        attended = dot(prob_b, values2).astype(BF16)
        acc[conv_rows + 512 * channels // 128 + j * 128 : conv_rows + 512 * channels // 128 + (j + 1) * 128, :] = dot_tn(
            attended, upstream[...]
        )
        grad_prob = dot_nt(g, values2)
        gs = []
        for h in range(2):
            gp = grad_prob[:, h * lanes : (h + 1) * lanes]
            gs.append(
                (probs[h] * (gp - jnp.sum(probs[h] * gp, axis=1, keepdims=True))).astype(BF16)
            )
        grad_s = jnp.concatenate(gs, axis=1)
        gv = dot_tn(prob_b, g)
        grad_kv[lanes:, cut] = jnp.where(low, gv[:lanes], gv[lanes:]).astype(BF16)
        gk = dot_tn(grad_s, q) * 0.125
        grad_kv[:lanes, cut] = jnp.where(low, gk[:lanes], gk[lanes:]).astype(BF16)
        gq = (dot(grad_s, keys2) * 0.125).astype(BF16)
        grad_query[:, cut] = gq
        acc[pl.ds(conv_rows + j, channels, stride=pairs), :] = dot_tn(feat[...], gq)

    outgoing = dot(placing, grad_kv[...]).astype(BF16)
    slot_send[...] = outgoing.reshape(dps, cap_rows, kv.shape[1])
    slot_copies = []
    for d in range(dps - 1, 0, -1):
        copy = send(slot_send.at[peers[d]], slot_recv.at[me], slot_sem, d, {"dp": peers[d]})
        copy.start()
        slot_copies.append(copy)
    slot_recv[me] = slot_send[me]

    grad_feat = upstream[...].astype(F32) + dot_nt(grad_query[...], query_w[...])
    v = pre[...]
    sig = jax.nn.sigmoid(v)
    grad_pre = (grad_feat * (sig * (1.0 + v * (1.0 - sig)))).astype(BF16)
    for a in range(3):
        acc[a * 9 * channels : (a + 1) * 9 * channels, :] = dot_tn(columns(a), grad_pre)

    if reduce_here:
        pad_rows = rep_send.shape[2]
        acc[acc.shape[0] - 8 :, :] = jnp.zeros((8, 128), F32)

        def chunk(p, s, r):
            start = pl.multiple_of(((p * subs + s) * 2 + r) * rows_dev, 8)
            return acc[pl.ds(start, pad_rows), :]

        rep_copies = []
        for half in range(2):
            s = (1 - sub) if half == 0 else sub
            for p in range(dps):
                rep_send[half, p] = chunk(p, s, 1 - rep).astype(BF16)
            copy = send(rep_send.at[half], rep_recv.at[half], rep_sem, half, {"rep": 1 - rep})
            copy.start()
            rep_copies.append(copy)
        rep_copies[0].wait()
        for p in range(dps):
            sub_send[p] = (chunk(p, 1 - sub, rep) + rep_recv[0, p].astype(F32)).astype(BF16)
        sub_copy = send(sub_send, sub_recv, sub_sem, 0, {"sub": 1 - sub})
        sub_copy.start()
        rep_copies[1].wait()
        for p in range(dps):
            part[p] = chunk(p, sub, rep) + rep_recv[1, p].astype(F32)
        sub_copy.wait()
        dp_copies = []
        for d in range(dps - 1, 0, -1):
            p = peers[d]
            dp_send[d - 1] = (part[p] + sub_recv[p].astype(F32)).astype(BF16)
            copy = send(dp_send.at[d - 1], dp_recv.at[d - 1], dp_sem, d, {"dp": p})
            copy.start()
            dp_copies.append(copy)
        total = part[me] + sub_recv[me].astype(F32)

    for copy in slot_copies:
        copy.wait()
    tile_out[...] = dot_tn(
        picks[...].reshape(place_rows, tiles * 16),
        slot_recv[...].reshape(place_rows, kv.shape[1]),
    )
    if reduce_here:
        for copy in dp_copies:
            copy.wait()
        for d in range(1, dps):
            total = total + dp_recv[d - 1].astype(F32)
        weight_out[...] = total[:rows_dev]
    else:
        weight_out[...] = acc[: weight_out.shape[0], :]


def per_device(
    fine,
    conv_weight,
    query_weight,
    out_weight,
    coarse_kv,
    key_bias,
    zone_ids,
    zone_counts,
    grad_out,
):
    strip_len, side, _, channels = fine.shape[1:]
    inner = query_weight.shape[1]
    tiles = coarse_kv.shape[1]
    slots = zone_ids.shape[1] * zone_ids.shape[2]
    dps, subs, reps = lax.axis_size("dp"), lax.axis_size("sub"), lax.axis_size("rep")
    cap = 2 * slots // dps
    cap_rows = cap * 16
    lanes = slots * 8
    planes = strip_len // 2
    cells = (side // 2) ** 2
    rows = planes * cells
    weight_rows = (27 * channels * channels + 2 * channels * inner) // 128
    devices = dps * subs * reps
    reduce_here = subs == 2 and weight_rows % (8 * devices) == 0
    rows_dev = weight_rows // devices if reduce_here else 16
    pad_rows = -(-rows_dev // 16) * 16
    bias_rows = jnp.tile(key_bias[0].astype(F32), (1, slots))
    ids_row = jnp.repeat(zone_ids[0].reshape(-1), 8).astype(F32)
    count_row = jnp.full((1, lanes), zone_counts[0, 0], F32)
    meta = jnp.concatenate(
        [bias_rows, ids_row[None], jnp.broadcast_to(count_row, (7, lanes))], axis=0
    )
    cfg = (dps, subs, tiles, cap, slots, rows_dev, reduce_here)
    weight_shape = (rows_dev, 128) if reduce_here else (weight_rows, 128)
    vmem = pl.BlockSpec(memory_space=pltpu.VMEM)
    weight_out, tile_out = pl.pallas_call(
        functools.partial(kernel, cfg),
        out_shape=(
            jax.ShapeDtypeStruct(weight_shape, F32),
            jax.ShapeDtypeStruct((tiles * 16, inner), F32),
        ),
        in_specs=[vmem] * 8,
        out_specs=(vmem, vmem),
        scratch_shapes=[
            pltpu.VMEM((side * side, channels), BF16),
            pltpu.VMEM((planes, cells, 9 * channels), BF16),
            pltpu.VMEM((planes + 1, cells, 9 * channels), BF16),
            pltpu.VMEM((rows, channels), F32),
            pltpu.VMEM((rows, channels), BF16),
            pltpu.VMEM((rows, inner), BF16),
            pltpu.VMEM((rows, inner), BF16),
            pltpu.VMEM((2 * lanes, inner), BF16),
            pltpu.VMEM((rows, inner), BF16),
            pltpu.VMEM((weight_rows + 8, 128), F32),
            pltpu.VMEM((dps, tiles + 8, lanes), F32),
            pltpu.VMEM((dps - 1, cap_rows, inner), BF16),
            pltpu.VMEM((dps, cap_rows, inner), BF16),
            pltpu.VMEM((dps, cap_rows, inner), BF16),
            pltpu.VMEM((dps, cap_rows, inner), BF16),
            pltpu.VMEM((dps, cap_rows, tiles * 16), BF16),
            pltpu.VMEM((2, dps, pad_rows, 128), BF16),
            pltpu.VMEM((2, dps, pad_rows, 128), BF16),
            pltpu.VMEM((dps, pad_rows, 128), BF16),
            pltpu.VMEM((dps, pad_rows, 128), BF16),
            pltpu.VMEM((dps, pad_rows, 128), F32),
            pltpu.VMEM((dps - 1, pad_rows, 128), BF16),
            pltpu.VMEM((dps - 1, pad_rows, 128), BF16),
            pltpu.SemaphoreType.DMA((2, 1)),
            pltpu.SemaphoreType.DMA((2, dps)),
            pltpu.SemaphoreType.DMA((2, dps)),
            pltpu.SemaphoreType.DMA((2, dps)),
            pltpu.SemaphoreType.DMA((2, 2)),
            pltpu.SemaphoreType.DMA((2, 1)),
            pltpu.SemaphoreType.DMA((2, dps)),
        ],
        compiler_params=pltpu.CompilerParams(
            collective_id=0, has_side_effects=True, vmem_limit_bytes=48 * 1024 * 1024
        ),
    )(
        fine[0].reshape(strip_len, side * side, channels),
        jnp.asarray(tap_selector(side), BF16),
        conv_weight.reshape(3, 9 * channels, channels),
        query_weight,
        out_weight,
        coarse_kv[0].reshape(tiles * 16, inner),
        meta,
        grad_out[0].reshape(rows, channels),
    )
    weight_grads = weight_out.reshape(-1)
    if not reduce_here:
        weight_grads = lax.psum_scatter(
            weight_grads, ("dp", "sub", "rep"), scatter_dimension=0, tiled=True
        )
    return (weight_grads, tile_out.reshape(1, tiles, 2, 8, inner))


def solution(mesh):
    in_specs = (
        P(("grp", "dp", "rep"), "sub", None, None, None),
        P(),
        P(),
        P(),
        P(("grp", "sub", "rep"), "dp", None, None, None),
        P(("grp", "sub", "rep"), "dp", None),
        P(("grp", "dp", "rep"), "sub", None),
        P(("grp", "dp", "rep"), "sub"),
        P(("grp", "dp", "rep"), "sub", None, None, None),
    )
    out_specs = (P(("grp", "dp", "sub", "rep")), P(("grp", "sub", "rep"), "dp", None, None, None))
    return jax.shard_map(
        per_device, mesh=mesh, in_specs=in_specs, out_specs=out_specs, check_vma=False
    )
```

time: 218 us -> 56.9 us (0.26)
  waiting for transfers between devices: 93.9 us -> 0 us
  Pallas kernels: 0 us -> 45.9 us
  matrix products: 38 us -> 0 us
  local copies, waits for them, and re-layouts: 32.8 us -> 7.89 us
  between operations: 16.4 us -> 1.36 us
  starting transfers between devices: 14.8 us -> 0 us
  blocking collectives: 13.8 us -> 0 us
  other arithmetic: 6.83 us -> 1.42 us
    unnamed x3 -> x0, waiting for transfers between devices: 78.6 us -> none
    pallas_call x0 -> x1, Pallas kernels: none -> 45.9 us  [per_device(): pl.pallas_call(functools.partial(kernel, cfg), out_shape=(jax.ShapeDtypeS...]
    dot_general x48 -> x0, matrix products: 34.6 us -> none  [the longest x9 8.56 us: per_device(): jnp.dot(prev_z, conv_weight[base], preferred_element_type=jnp.float32)]
    all_to_all x2 -> x0, waiting for transfers between devices: 15.3 us -> none  [the longest x1 15.3 us: per_device(): lax.all_to_all(outgoing, 'dp', split_axis=0, concat_axis=0, tiled=True)]
    all_gather x1 -> x0, blocking collectives: 13.8 us -> none  [per_device(): lax.all_gather(key_bias[0], 'dp', axis=0, tiled=True)]
    all_to_all x2 -> x0, starting transfers between devices: 10.8 us -> none  [the longest x1 6.32 us: per_device(): lax.all_to_all(request, 'dp', split_axis=0, concat_axis=0, tiled=True)]
    another operation x9 -> x3, local copies, waits for them, and re-layouts: 7.35 us -> 0.06 us  [the longest x2 0.06 us: per_device(): bias_rows = jnp.tile(key_bias[0].astype(F32), (1, slots))]
    ppermute x1 -> x0, starting transfers between devices: 4.01 us -> none  [from_behind(): return lax.ppermute(block, axis, route)]
  transfers between devices with their start and end apart: 5 -> 0, of which waited for: 2 -> 0; matrix products, arithmetic and copies ran while one was open for 34% -> 0% of each run, Pallas kernels for 0% -> 0%
where the time goes in v1:
time: 56.9 us; the launch traced here: 56.6 us
  Pallas kernels  45.9 us (81%)
  local copies, waits for them, and re-layouts  7.89 us (14%)
  other arithmetic  1.42 us (2%)
  between operations  1.36 us (2%)
    pallas_call x1, Pallas kernels, per_device(): pl.pallas_call(functools.partial(kernel, cfg), out_shape=(jax.ShapeDtypeS...  45.9 us
    unnamed x16, local copies, waits for them, and re-layouts  7.6 us

profile of v1, /device:TPU:0, one launch (start us, length us, event | category | flops | bytes accessed | tf_op | source)
XLA Modules:
  0.0 56.6 jit_solution(13919795792019826095)
XLA Ops:
  0.6 0.0 copy-start.4
  1.3 0.1 pad.2.clone
  1.4 0.7 %convert_bitcast_fusion = f32[16]{0:T(128)S(1)} fusion(s32[1,1,16]{2,1,0:T(1,128)} %param.16), kind=kLoop, calls=%fused_computation.3 | loop fusion | flops 16 | bytes 128 | tf_op jit(solution)/shard_map/convert_element_type | solution.py:371
  2.1 0.7 %bitcast_convert_fusion = f32[16,8]{0,1:T(8,128)S(1)} fusion(bf16[1,16,8]{1,2,0:T(8,128)(2,1)} %param.15), kind=kLoop, calls=%fused_computation.2 | loop fusion | flops 128 | bytes 768 | tf_op jit(solution)/shard_map/convert_element_type | solution.py:370
  2.7 0.1 broadcast_in_dim.4
  2.8 0.1 convert_element_type.37
  2.9 0.1 copy.13
  3.0 0.1 maximum_maximum_fusion.meta
  3.0 0.0 copy-done.4
  3.1 0.0 copy-start
  3.1 1.2 %copy-done = bf16[1,16,16,16,128]{4,3,2,1,0:T(8,128)(2,1)S(1)} copy-done((bf16[1,16,16,16,128]{4,3,2,1,0:T(8,128)(2,1)S(1)}, bf16[1,16,16,16,128]{4,3,2,1,0:T(8,128)(2,1)}, u32[]{:S(2)}) %copy-start) | copy-done | bytes 1048600
  4.3 0.0 copy-start.1
  4.3 1.2 %copy-done.1 = bf16[27,128,128]{2,1,0:T(8,128)(2,1)S(1)} copy-done((bf16[27,128,128]{2,1,0:T(8,128)(2,1)S(1)}, bf16[27,128,128]{2,1,0:T(8,128)(2,1)}, u32[]{:S(2)}) %copy-start.1) | copy-done | bytes 884760
  5.5 0.0 copy-start.2
  5.5 1.0 %copy-done.2 = bf16[576,256]{1,0:T(8,128)(2,1)S(1)} copy-done((bf16[576,256]{1,0:T(8,128)(2,1)S(1)}, bf16[576,256]{1,0:T(8,128)(2,1)}, u32[]{:S(2)}) %copy-start.2) | copy-done | bytes 294936
  6.4 0.0 copy-start.3
  6.4 0.9 %copy-done.3 = bf16[1,16,2,8,512]{4,3,2,1,0:T(8,128)(2,1)S(1)} copy-done((bf16[1,16,2,8,512]{4,3,2,1,0:T(8,128)(2,1)S(1)}, bf16[1,16,2,8,512]{4,3,2,1,0:T(8,128)(2,1)}, u32[]{:S(2)}) %copy-start.3) | copy-done | bytes 262168
  7.4 0.0 copy-start.5
  7.4 0.9 %copy-done.5 = bf16[512,128]{1,0:T(8,128)(2,1)S(1)} copy-done((bf16[512,128]{1,0:T(8,128)(2,1)S(1)}, bf16[512,128]{1,0:T(8,128)(2,1)}, u32[]{:S(2)}) %copy-start.5) | copy-done | bytes 131096
  8.3 0.0 copy-start.6
  8.3 0.9 %copy-done.6 = bf16[1,8,8,8,128]{4,3,2,1,0:T(8,128)(2,1)S(1)} copy-done((bf16[1,8,8,8,128]{4,3,2,1,0:T(8,128)(2,1)S(1)}, bf16[1,8,8,8,128]{4,3,2,1,0:T(8,128)(2,1)}, u32[]{:S(2)}) %copy-start.6) | copy-done | bytes 131096
  9.2 45.9 %shard_map.113 = (f32[280,128]{1,0:T(8,128)S(1)}, f32[256,512]{1,0:T(8,128)S(1)}) custom-call(bf16[16,256,128]{2,1,0:T(8,128)(2,1)S(1)} %bitcast.14, bf16[576,256]{1,0:T(8,128)(2,1)S(1)} %copy-done.2, bf16[3,1152,128]{2,1,0:T(8,128)(2,1)S(1)} %bitcast.15, bf16[128,512]{1,0:T(8,128)(2,1)S(1)} %copy-done.4, bf16[512,128]{1,0:T(8,128)(2,1)S(1)} %copy-done.5, ...), custom_call_target="tpu_custom_call" | custom-call | tf_op jit(solution)/shard_map/pallas_call | solution.py:379
  55.1 0.7 %copy.17 = f32[35840]{0:T(1024)} copy(f32[35840]{0:T(1024)S(1)} %bitcast.18) | data formatting | bytes 286720
  55.8 0.8 %copy.18 = f32[1,16,2,8,512]{4,3,2,1,0:T(8,128)} copy(f32[1,16,2,8,512]{4,3,2,1,0:T(8,128)S(1)} %bitcast.16) | data formatting | bytes 1048576
  (2 shorter events, 0.0 us)
Async XLA Ops:
  0.6 2.4 %copy-start.4 = (bf16[128,512]{1,0:T(8,128)(2,1)S(1)}, bf16[128,512]{1,0:T(8,128)(2,1)}, u32[]{:S(2)}) copy-start(bf16[128,512]{1,0:T(8,128)(2,1)} %query_w.1) | copy-start | bytes 393220
  3.1 1.2 %copy-start = (bf16[1,16,16,16,128]{4,3,2,1,0:T(8,128)(2,1)S(1)}, bf16[1,16,16,16,128]{4,3,2,1,0:T(8,128)(2,1)}, u32[]{:S(2)}) copy-start(bf16[1,16,16,16,128]{4,3,2,1,0:T(8,128)(2,1)} %param.10) | copy-start | bytes 3145732
  4.3 1.2 %copy-start.1 = (bf16[27,128,128]{2,1,0:T(8,128)(2,1)S(1)}, bf16[27,128,128]{2,1,0:T(8,128)(2,1)}, u32[]{:S(2)}) copy-start(bf16[27,128,128]{2,1,0:T(8,128)(2,1)} %param.11) | copy-start | bytes 2654212
  5.5 1.0 %copy-start.2 = (bf16[576,256]{1,0:T(8,128)(2,1)S(1)}, bf16[576,256]{1,0:T(8,128)(2,1)}, u32[]{:S(2)}) copy-start(bf16[576,256]{1,0:T(8,128)(2,1)} %constant.2.clone.selector) | copy-start | bytes 884740
  6.4 0.9 %copy-start.3 = (bf16[1,16,2,8,512]{4,3,2,1,0:T(8,128)(2,1)S(1)}, bf16[1,16,2,8,512]{4,3,2,1,0:T(8,128)(2,1)}, u32[]{:S(2)}) copy-start(bf16[1,16,2,8,512]{4,3,2,1,0:T(8,128)(2,1)} %param.14) | copy-start | bytes 786436
  7.4 0.9 %copy-start.5 = (bf16[512,128]{1,0:T(8,128)(2,1)S(1)}, bf16[512,128]{1,0:T(8,128)(2,1)}, u32[]{:S(2)}) copy-start(bf16[512,128]{1,0:T(8,128)(2,1)} %out_w.1) | copy-start | bytes 393220
  8.3 0.9 %copy-start.6 = (bf16[1,8,8,8,128]{4,3,2,1,0:T(8,128)(2,1)S(1)}, bf16[1,8,8,8,128]{4,3,2,1,0:T(8,128)(2,1)}, u32[]{:S(2)}) copy-start(bf16[1,8,8,8,128]{4,3,2,1,0:T(8,128)(2,1)} %param.18) | copy-start | bytes 393220

commit v2 on v1

v2 whole, which is shorter than its diff:
```python
import functools

import jax
import jax.numpy as jnp
import numpy as np
from jax import lax
from jax.experimental import pallas as pl
from jax.experimental.pallas import tpu as pltpu
from jax.sharding import PartitionSpec as P

HEADS = 8
MESH = pl.DeviceIdType.MESH
F32 = jnp.float32
BF16 = jnp.bfloat16


def dot(a, b):
    return jnp.dot(a, b, preferred_element_type=F32)


def dot_nt(a, b):
    return lax.dot_general(a, b, (((1,), (1,)), ((), ())), preferred_element_type=F32)


def dot_tn(a, b):
    return lax.dot_general(a, b, (((0,), (0,)), ((), ())), preferred_element_type=F32)


def iota(shape, dim):
    return lax.broadcasted_iota(jnp.int32, shape, dim)


def tap_selector(side):
    half = side // 2
    sel = np.zeros((9, half, half, side, side), np.float32)
    for b in range(3):
        for c in range(3):
            for y in range(half):
                for z in range(half):
                    yy, zz = 2 * y + b - 1, 2 * z + c - 1
                    if yy >= 0 and zz >= 0:
                        sel[b * 3 + c, y, z, yy, zz] = 1.0
    return sel.reshape(9 * half * half, side * side)


def kernel(
    cfg,
    fine_hbm,
    selector_hbm,
    conv_w_hbm,
    query_w_hbm,
    out_w_hbm,
    kv_hbm,
    bias_hbm,
    ids_hbm,
    count_hbm,
    upstream_hbm,
    weight_out,
    tile_out,
    fine,
    selector,
    conv_w,
    query_w,
    out_w,
    kv,
    bias_in,
    ids_in,
    count_in,
    upstream,
    meta,
    halo,
    t_even,
    t_odd,
    pre,
    feat,
    query,
    grad_att,
    grad_query,
    acc,
    metas,
    kv_send,
    kv_recv,
    slot_send,
    slot_recv,
    picks,
    rep_send,
    rep_recv,
    sub_send,
    sub_recv,
    part,
    dp_send,
    dp_recv,
    load_sem,
    halo_sem,
    meta_sem,
    kv_sem,
    slot_sem,
    rep_sem,
    sub_sem,
    dp_sem,
):
    dps, subs, tiles, cap, slots, rows_dev, reduce_here = cfg
    me = lax.axis_index("dp")
    sub = lax.axis_index("sub")
    rep = lax.axis_index("rep")
    cap_rows = cap * 16
    planes = t_even.shape[0]
    cells = t_even.shape[1]
    channels = fine.shape[2]
    lanes = slots * 8
    pairs = query.shape[1] // 128
    place_rows = dps * cap_rows
    peers = [lax.rem(me + d, dps) for d in range(dps)]

    barrier = pltpu.get_barrier_semaphore()
    greeted = 0
    for d in range(1, dps):
        pl.semaphore_signal(barrier, inc=1, device_id={"dp": peers[d]}, device_id_type=MESH)
        greeted += 1
    for step in (1, subs - 1) if subs > 2 else (1,):
        pl.semaphore_signal(
            barrier, inc=1, device_id={"sub": lax.rem(sub + step, subs)}, device_id_type=MESH
        )
        greeted += 1
    pl.semaphore_signal(barrier, inc=1, device_id={"rep": 1 - rep}, device_id_type=MESH)
    greeted += 1

    loads = []
    for i, (src, dst) in enumerate(
        (
            (ids_hbm, ids_in),
            (bias_hbm, bias_in),
            (count_hbm, count_in),
            (selector_hbm, selector),
            (fine_hbm, fine),
            (kv_hbm, kv),
            (upstream_hbm, upstream),
            (out_w_hbm, out_w),
            (conv_w_hbm, conv_w),
            (query_w_hbm, query_w),
        )
    ):
        copy = pltpu.make_async_copy(src, dst, load_sem.at[i])
        copy.start()
        loads.append(copy)

    def send(src, dst, sems, index, where):
        return pltpu.make_async_remote_copy(
            src_ref=src,
            dst_ref=dst,
            send_sem=sems.at[0, index],
            recv_sem=sems.at[1, index],
            device_id=where,
            device_id_type=MESH,
        )

    for i in range(3):
        loads[i].wait()
    spread = jnp.where(iota((slots, lanes), 0) == iota((slots, lanes), 1) // 8, 1.0, 0.0)
    ids_row = dot(ids_in[...].astype(BF16), spread.astype(BF16))
    key_of = jnp.where(iota((8, lanes), 0) == iota((8, lanes), 1) % 8, 1.0, 0.0)
    meta[:tiles, :] = dot_tn(bias_in[...], key_of.astype(BF16))
    meta[tiles:, :] = jnp.broadcast_to(ids_row, (8, lanes))
    metas[me] = meta[...]
    count = count_in[...].astype(F32)

    pl.semaphore_wait(barrier, greeted)
    meta_copies = [
        send(meta, metas.at[me], meta_sem, d, {"dp": peers[d]}) for d in range(1, dps)
    ]
    for copy in meta_copies:
        copy.start()
    loads[3].wait()
    loads[4].wait()
    halo_copy = send(
        fine.at[2 * planes - 1], halo, halo_sem, 0, {"sub": lax.rem(sub + 1, subs)}
    )
    halo_copy.start()

    def spread_taps(found, target, index):
        for tap in range(9):
            target[index, :, tap * channels : (tap + 1) * channels] = found[
                tap * cells : (tap + 1) * cells
            ]

    def unfold(i, carry):
        pair = jnp.concatenate([fine[2 * i], fine[2 * i + 1]], axis=1)
        found = dot(selector[...], pair).astype(BF16)
        spread_taps(found[:, :channels], t_even, i)
        spread_taps(found[:, channels:], t_odd, i + 1)
        return carry

    early = planes // 2
    lax.fori_loop(0, early, unfold, 0)

    def slot_dest(ids_row):
        owner_row = jnp.floor(ids_row * (1.0 / tiles))
        owner_col = jnp.transpose(jnp.broadcast_to(owner_row, (lanes, lanes)))
        earlier = (iota((lanes, lanes), 0) // 8) < (iota((lanes, lanes), 1) // 8)
        same = jnp.where((owner_col == owner_row) & earlier, 1.0, 0.0)
        rank = jnp.sum(same, axis=0, keepdims=True) * 0.125
        return owner_row * cap + rank

    me_f = me.astype(F32)

    def picker(ids_row):
        dest = slot_dest(ids_row)
        slot_row = (iota((cap_rows, lanes), 0) // 16).astype(F32) + me_f * cap
        first = (iota((cap_rows, lanes), 1) % 8) == 0
        by_slot = jnp.where((slot_row == dest) & first, 1.0, 0.0).astype(BF16)
        tile_row = (iota((tiles * 16, lanes), 0) // 16).astype(F32) + me_f * tiles
        by_tile = jnp.where(tile_row == ids_row, 1.0, 0.0).astype(BF16)
        matched = dot_nt(by_slot, by_tile)
        unit = (iota(matched.shape, 0) % 16) == (iota(matched.shape, 1) % 16)
        return jnp.where(unit, matched, 0.0).astype(BF16)

    for copy in meta_copies:
        copy.wait()
    loads[5].wait()
    for p in range(dps):
        picks[p] = picker(metas[p, tiles : tiles + 1, :])
    kv_copies = []
    for j in range(pairs):
        cut = slice(j * 128, (j + 1) * 128)
        chosen = dot(picks[...].reshape(place_rows, tiles * 16), kv[:, cut]).astype(BF16)
        kv_send[j] = chosen.reshape(dps, cap_rows, 128)
        group = []
        for d in range(dps - 1, 0, -1):
            copy = send(
                kv_send.at[j, peers[d]],
                kv_recv.at[j, me],
                kv_sem,
                j * dps + d,
                {"dp": peers[d]},
            )
            copy.start()
            group.append(copy)
        kv_copies.append(group)
        kv_recv[j, me] = kv_send[j, me]

    lax.fori_loop(early, planes, unfold, 0)
    halo_copy.wait()
    edge = dot(selector[...], halo[...])
    edge = jnp.where(sub > 0, edge, 0.0).astype(BF16)
    spread_taps(edge, t_odd, 0)

    row_count = planes * cells

    def columns(a):
        if a == 1:
            return t_even[...].reshape(row_count, 9 * channels)
        start = a // 2
        return t_odd[start : start + planes].reshape(row_count, 9 * channels)

    for i in range(6, 10):
        loads[i].wait()
    value = dot(columns(0), conv_w[0]) + dot(columns(1), conv_w[1]) + dot(columns(2), conv_w[2])
    pre[...] = value
    feat[...] = (value * jax.nn.sigmoid(value)).astype(BF16)
    query[...] = dot(feat[...], query_w[...]).astype(BF16)
    grad_att[...] = dot_nt(upstream[...], out_w[...]).astype(BF16)

    ids_row = meta[tiles : tiles + 1, :]
    dest = slot_dest(ids_row)
    dest2 = jnp.concatenate([dest, dest], axis=1)
    row_i = iota((place_rows, 2 * lanes), 0)
    lane_i = iota((place_rows, 2 * lanes), 1)
    fits = ((row_i // 16).astype(F32) == dest2) & (
        (row_i % 16) == (lane_i // lanes) * 8 + lane_i % 8
    )
    placing = jnp.where(fits, 1.0, 0.0).astype(BF16)

    bias = jnp.zeros((1, lanes), F32)
    for owner in range(dps):
        tile_row = iota((tiles, lanes), 0).astype(F32) + float(owner * tiles)
        bias = bias + jnp.sum(
            jnp.where(tile_row == ids_row, metas[owner, :tiles, :], 0.0), axis=0, keepdims=True
        )
    lane_slot = (iota((1, lanes), 1) // 8).astype(F32)
    bias = jnp.where(lane_slot < count, bias, -jnp.inf)

    low = iota((lanes, 128), 1) < 64
    conv_rows = 27 * channels
    out_rows = conv_rows + pairs * channels
    slot_copies = []
    for j in range(pairs):
        for copy in kv_copies[j]:
            copy.wait()
        kv_pair = dot_tn(placing, kv_recv[j].reshape(place_rows, 128)).astype(BF16)
        cut = slice(j * 128, (j + 1) * 128)
        keys = kv_pair[:lanes]
        values = kv_pair[lanes:]
        none = jnp.zeros_like(keys)
        keys2 = jnp.concatenate(
            [jnp.where(low, keys, none), jnp.where(low, none, keys)], axis=0
        )
        values2 = jnp.concatenate(
            [jnp.where(low, values, none), jnp.where(low, none, values)], axis=0
        )
        q = query[:, cut]
        g = grad_att[:, cut]
        scores = dot_nt(q, keys2) * 0.125
        grad_prob = dot_nt(g, values2)
        probs = []
        gs = []
        for h in range(2):
            s = scores[:, h * lanes : (h + 1) * lanes] + bias
            e = jnp.exp(s - jnp.max(s, axis=1, keepdims=True))
            prob = e * (1.0 / jnp.sum(e, axis=1, keepdims=True))
            gp = grad_prob[:, h * lanes : (h + 1) * lanes]
            probs.append(prob.astype(BF16))
            gs.append((prob * (gp - jnp.sum(prob * gp, axis=1, keepdims=True))).astype(BF16))
        prob_b = jnp.concatenate(probs, axis=1)
        grad_s = jnp.concatenate(gs, axis=1)
        gv = dot_tn(prob_b, g)
        gk = dot_tn(grad_s, q) * 0.125
        grad_pair = jnp.concatenate(
            [
                jnp.where(low, gk[:lanes], gk[lanes:]).astype(BF16),
                jnp.where(low, gv[:lanes], gv[lanes:]).astype(BF16),
            ],
            axis=0,
        )
        slot_send[j] = dot(placing, grad_pair).astype(BF16).reshape(dps, cap_rows, 128)
        group = []
        for d in range(dps - 1, 0, -1):
            copy = send(
                slot_send.at[j, peers[d]],
                slot_recv.at[j, me],
                slot_sem,
                j * dps + d,
                {"dp": peers[d]},
            )
            copy.start()
            group.append(copy)
        slot_copies.append(group)
        slot_recv[j, me] = slot_send[j, me]
        attended = dot(prob_b, values2).astype(BF16)
        acc[out_rows + j * 128 : out_rows + (j + 1) * 128, :] = dot_tn(attended, upstream[...])
        gq = (dot(grad_s, keys2) * 0.125).astype(BF16)
        grad_query[:, cut] = gq
        acc[pl.ds(conv_rows + j, channels, stride=pairs), :] = dot_tn(feat[...], gq)

    grad_feat = upstream[...].astype(F32) + dot_nt(grad_query[...], query_w[...])
    v = pre[...]
    sig = jax.nn.sigmoid(v)
    grad_pre = (grad_feat * (sig * (1.0 + v * (1.0 - sig)))).astype(BF16)

    def conv_grad(a):
        acc[a * 9 * channels : (a + 1) * 9 * channels, :] = dot_tn(columns(a), grad_pre)

    def scatter_tiles(j):
        for copy in slot_copies[j]:
            copy.wait()
        tile_out[:, j * 128 : (j + 1) * 128] = dot_tn(
            picks[...].reshape(place_rows, tiles * 16), slot_recv[j].reshape(place_rows, 128)
        )

    if not reduce_here:
        for a in range(3):
            conv_grad(a)
        for j in range(pairs):
            scatter_tiles(j)
        weight_out[...] = acc[: weight_out.shape[0], :]
        return

    pad_rows = rep_send.shape[2]
    acc[acc.shape[0] - 8 :, :] = jnp.zeros((8, 128), F32)

    def chunk(p, s, r):
        start = pl.multiple_of(((p * subs + s) * 2 + r) * rows_dev, 8)
        return acc[pl.ds(start, pad_rows), :]

    rep_copies = [
        send(rep_send.at[p], rep_recv.at[p], rep_sem, p, {"rep": 1 - rep}) for p in range(dps)
    ]
    sub_copies = [
        send(sub_send.at[p], sub_recv.at[p], sub_sem, p, {"sub": 1 - sub}) for p in range(dps)
    ]

    def start_rep(p):
        rep_send[p, 0] = chunk(p, 1 - sub, 1 - rep).astype(BF16)
        rep_send[p, 1] = chunk(p, sub, 1 - rep).astype(BF16)
        rep_copies[p].start()

    def start_sub(p):
        rep_copies[p].wait()
        sub_send[p] = (chunk(p, 1 - sub, rep) + rep_recv[p, 0].astype(F32)).astype(BF16)
        sub_copies[p].start()
        part[p] = chunk(p, sub, rep) + rep_recv[p, 1].astype(F32)

    def start_dp(p):
        sub_copies[p].wait()
        part[p] = part[p] + sub_recv[p].astype(F32)

        @pl.when(me != p)
        def _():
            dp_send[p] = part[p].astype(BF16)
            d = lax.rem(p - me + dps, dps)
            send(dp_send.at[p], dp_recv.at[d], dp_sem, d, {"dp": p}).start()

    done_rep = done_sub = 0
    for a in range(3):
        conv_grad(a)
        ready = dps if a == 2 else (a + 1) * 9 * channels // (4 * rows_dev)
        if a > 0 and done_sub < done_rep:
            start_sub(done_sub)
            done_sub += 1
        while done_rep < ready:
            start_rep(done_rep)
            done_rep += 1
    for p in range(dps):
        if done_sub < dps:
            start_sub(done_sub)
            done_sub += 1
        start_dp(p)
    for j in range(pairs):
        scatter_tiles(j)
    total = part[me]
    for d in range(1, dps):
        send(dp_send.at[peers[d]], dp_recv.at[d], dp_sem, d, {"dp": peers[d]}).wait()
        total = total + dp_recv[d].astype(F32)
    weight_out[...] = total[:rows_dev]


def per_device(
    fine,
    conv_weight,
    query_weight,
    out_weight,
    coarse_kv,
    key_bias,
    zone_ids,
    zone_counts,
    grad_out,
):
    strip_len, side, _, channels = fine.shape[1:]
    inner = query_weight.shape[1]
    tiles = coarse_kv.shape[1]
    slots = zone_ids.shape[1] * zone_ids.shape[2]
    dps, subs, reps = lax.axis_size("dp"), lax.axis_size("sub"), lax.axis_size("rep")
    cap = 2 * slots // dps
    cap_rows = cap * 16
    lanes = slots * 8
    planes = strip_len // 2
    cells = (side // 2) ** 2
    rows = planes * cells
    weight_rows = (27 * channels * channels + 2 * channels * inner) // 128
    devices = dps * subs * reps
    reduce_here = subs == 2 and weight_rows % (8 * devices) == 0
    rows_dev = weight_rows // devices if reduce_here else 16
    pad_rows = -(-rows_dev // 16) * 16
    cfg = (dps, subs, tiles, cap, slots, rows_dev, reduce_here)
    weight_shape = (rows_dev, 128) if reduce_here else (weight_rows, 128)
    vmem = pl.BlockSpec(memory_space=pltpu.VMEM)
    pairs = inner // 128
    hbm = pl.BlockSpec(memory_space=pltpu.HBM)
    weight_out, tile_out = pl.pallas_call(
        functools.partial(kernel, cfg),
        out_shape=(
            jax.ShapeDtypeStruct(weight_shape, F32),
            jax.ShapeDtypeStruct((tiles * 16, inner), F32),
        ),
        in_specs=[hbm] * 10,
        out_specs=(vmem, vmem),
        scratch_shapes=[
            pltpu.VMEM((strip_len, side * side, channels), BF16),
            pltpu.VMEM((9 * cells, side * side), BF16),
            pltpu.VMEM((3, 9 * channels, channels), BF16),
            pltpu.VMEM((channels, inner), BF16),
            pltpu.VMEM((inner, channels), BF16),
            pltpu.VMEM((tiles * 16, inner), BF16),
            pltpu.VMEM((8, tiles), BF16),
            pltpu.VMEM((1, slots), jnp.int32),
            pltpu.VMEM((1, 1), jnp.int32),
            pltpu.VMEM((rows, channels), BF16),
            pltpu.VMEM((tiles + 8, lanes), F32),
            pltpu.VMEM((side * side, channels), BF16),
            pltpu.VMEM((planes, cells, 9 * channels), BF16),
            pltpu.VMEM((planes + 1, cells, 9 * channels), BF16),
            pltpu.VMEM((rows, channels), F32),
            pltpu.VMEM((rows, channels), BF16),
            pltpu.VMEM((rows, inner), BF16),
            pltpu.VMEM((rows, inner), BF16),
            pltpu.VMEM((rows, inner), BF16),
            pltpu.VMEM((weight_rows + 8, 128), F32),
            pltpu.VMEM((dps, tiles + 8, lanes), F32),
            pltpu.VMEM((pairs, dps, cap_rows, 128), BF16),
            pltpu.VMEM((pairs, dps, cap_rows, 128), BF16),
            pltpu.VMEM((pairs, dps, cap_rows, 128), BF16),
            pltpu.VMEM((pairs, dps, cap_rows, 128), BF16),
            pltpu.VMEM((dps, cap_rows, tiles * 16), BF16),
            pltpu.VMEM((dps, 2, pad_rows, 128), BF16),
            pltpu.VMEM((dps, 2, pad_rows, 128), BF16),
            pltpu.VMEM((dps, pad_rows, 128), BF16),
            pltpu.VMEM((dps, pad_rows, 128), BF16),
            pltpu.VMEM((dps, pad_rows, 128), F32),
            pltpu.VMEM((dps, pad_rows, 128), BF16),
            pltpu.VMEM((dps, pad_rows, 128), BF16),
            pltpu.SemaphoreType.DMA((10,)),
            pltpu.SemaphoreType.DMA((2, 1)),
            pltpu.SemaphoreType.DMA((2, dps)),
            pltpu.SemaphoreType.DMA((2, pairs * dps)),
            pltpu.SemaphoreType.DMA((2, pairs * dps)),
            pltpu.SemaphoreType.DMA((2, dps)),
            pltpu.SemaphoreType.DMA((2, dps)),
            pltpu.SemaphoreType.DMA((2, dps)),
        ],
        compiler_params=pltpu.CompilerParams(
            collective_id=0, has_side_effects=True, vmem_limit_bytes=64 * 1024 * 1024 - 256 * 1024
        ),
    )(
        fine[0].reshape(strip_len, side * side, channels),
        jnp.asarray(tap_selector(side), BF16),
        conv_weight.reshape(3, 9 * channels, channels),
        query_weight,
        out_weight,
        coarse_kv[0].reshape(tiles * 16, inner),
        key_bias[0].T,
        zone_ids[0].reshape(1, slots),
        zone_counts[:, :1],
        grad_out[0].reshape(rows, channels),
    )
    weight_grads = weight_out.reshape(-1)
    if not reduce_here:
        weight_grads = lax.psum_scatter(
            weight_grads, ("dp", "sub", "rep"), scatter_dimension=0, tiled=True
        )
    return (weight_grads, tile_out.reshape(1, tiles, 2, 8, inner))


def solution(mesh):
    in_specs = (
        P(("grp", "dp", "rep"), "sub", None, None, None),
        P(),
        P(),
        P(),
        P(("grp", "sub", "rep"), "dp", None, None, None),
        P(("grp", "sub", "rep"), "dp", None),
        P(("grp", "dp", "rep"), "sub", None),
        P(("grp", "dp", "rep"), "sub"),
        P(("grp", "dp", "rep"), "sub", None, None, None),
    )
    out_specs = (P(("grp", "dp", "sub", "rep")), P(("grp", "sub", "rep"), "dp", None, None, None))
    return jax.shard_map(
        per_device, mesh=mesh, in_specs=in_specs, out_specs=out_specs, check_vma=False
    )
```

time: 56.9 us -> 49.3 us (0.87)
  the two profiles are of different devices: /device:TPU:0 before, /device:TPU:28 now
where the time goes in v2:
time: 49.3 us; the launch traced here: 49.1 us
  Pallas kernels  44.4 us (90%)
  local copies, waits for them, and re-layouts  3.46 us (7%)
  between operations  1.29 us (3%)
    pallas_call x1, Pallas kernels, per_device(): pl.pallas_call(functools.partial(kernel, cfg), out_shape=(jax.ShapeDtypeS...  44.4 us
    unnamed x2, local copies, waits for them, and re-layouts  3.46 us

profile of v2, /device:TPU:28, one launch (start us, length us, event | category | flops | bytes accessed | tf_op | source)
XLA Modules:
  0.0 49.1 jit_solution(4132644305570163325)
XLA Ops:
  1.3 44.4 %shard_map.113 = (f32[280,128]{1,0:T(8,128)}, f32[256,512]{1,0:T(8,128)}) custom-call(bf16[16,256,128]{2,1,0:T(8,128)(2,1)} %bitcast.10, bf16[576,256]{1,0:T(8,128)(2,1)} %constant.2.clone.selector_hbm, bf16[3,1152,128]{2,1,0:T(8,128)(2,1)} %bitcast.11, bf16[128,512]{1,0:T(8,128)(2,1)} %query_w_hbm.1, bf16[512,128]{1,0:T(8,128)(2,1)} %out_w_hbm.1, ...), custom_call_target="tpu_custom_call" | custom-call | tf_op jit(solution)/shard_map/pallas_call | solution.py:458
  45.6 1.6 %copy.15 = f32[35840]{0:T(1024)} copy(f32[35840]{0:T(1024)} %bitcast.14) | data formatting | bytes 286720
  47.2 1.9 %copy.16 = f32[1,16,2,8,512]{4,3,2,1,0:T(8,128)} copy(f32[1,16,2,8,512]{4,3,2,1,0:T(8,128)} %bitcast.12) | data formatting | bytes 1048576

commit v3 on v2

--- a/solution.py
+++ b/solution.py
@@ -283,9 +283,27 @@
     conv_rows = 27 * channels
     out_rows = conv_rows + pairs * channels
     slot_copies = []
+
+    def start_slots(j):
+        group = []
+        for d in range(dps - 1, 0, -1):
+            copy = send(
+                slot_send.at[j, peers[d]],
+                slot_recv.at[j, me],
+                slot_sem,
+                j * dps + d,
+                {"dp": peers[d]},
+            )
+            copy.start()
+            group.append(copy)
+        slot_copies.append(group)
+
     for j in range(pairs):
         for copy in kv_copies[j]:
             copy.wait()
+        if j == pairs - 1:
+            for i in range(pairs - 1):
+                start_slots(i)
         kv_pair = dot_tn(placing, kv_recv[j].reshape(place_rows, 128)).astype(BF16)
         cut = slice(j * 128, (j + 1) * 128)
         keys = kv_pair[:lanes]
@@ -322,18 +340,8 @@
             axis=0,
         )
         slot_send[j] = dot(placing, grad_pair).astype(BF16).reshape(dps, cap_rows, 128)
-        group = []
-        for d in range(dps - 1, 0, -1):
-            copy = send(
-                slot_send.at[j, peers[d]],
-                slot_recv.at[j, me],
-                slot_sem,
-                j * dps + d,
-                {"dp": peers[d]},
-            )
-            copy.start()
-            group.append(copy)
-        slot_copies.append(group)
+        if j == pairs - 1:
+            start_slots(j)
         slot_recv[j, me] = slot_send[j, me]
         attended = dot(prob_b, values2).astype(BF16)
         acc[out_rows + j * 128 : out_rows + (j + 1) * 128, :] = dot_tn(attended, upstream[...])
@@ -409,10 +417,10 @@
         while done_rep < ready:
             start_rep(done_rep)
             done_rep += 1
-    for p in range(dps):
-        if done_sub < dps:
-            start_sub(done_sub)
-            done_sub += 1
+    late = list(range(done_sub, dps))[::-1]
+    for p in late:
+        start_sub(p)
+    for p in list(range(done_sub)) + late:
         start_dp(p)
     for j in range(pairs):
         scatter_tiles(j)

time: 49.3 us -> 45.1 us (0.915)
  the two profiles are of different devices: /device:TPU:28 before, /device:TPU:0 now
where the time goes in v3:
time: 45.1 us; the launch traced here: 44.5 us
  Pallas kernels  39.7 us (88%)
  local copies, waits for them, and re-layouts  3.46 us (8%)
  between operations  1.29 us (3%)
    pallas_call x1, Pallas kernels, per_device(): pl.pallas_call(functools.partial(kernel, cfg), out_shape=(jax.ShapeDtypeS...  39.7 us
    unnamed x2, local copies, waits for them, and re-layouts  3.46 us

profile of v3, /device:TPU:0, one launch (start us, length us, event | category | flops | bytes accessed | tf_op | source)
XLA Modules:
  0.0 44.5 jit_solution(13616819817394460370)
XLA Ops:
  1.3 39.7 %shard_map.113 = (f32[280,128]{1,0:T(8,128)}, f32[256,512]{1,0:T(8,128)}) custom-call(bf16[16,256,128]{2,1,0:T(8,128)(2,1)} %bitcast.10, bf16[576,256]{1,0:T(8,128)(2,1)} %constant.2.clone.selector_hbm, bf16[3,1152,128]{2,1,0:T(8,128)(2,1)} %bitcast.11, bf16[128,512]{1,0:T(8,128)(2,1)} %query_w_hbm.1, bf16[512,128]{1,0:T(8,128)(2,1)} %out_w_hbm.1, ...), custom_call_target="tpu_custom_call" | custom-call | tf_op jit(solution)/shard_map/pallas_call | solution.py:466
  41.0 1.6 %copy.15 = f32[35840]{0:T(1024)} copy(f32[35840]{0:T(1024)} %bitcast.14) | data formatting | bytes 286720
  42.6 1.9 %copy.16 = f32[1,16,2,8,512]{4,3,2,1,0:T(8,128)} copy(f32[1,16,2,8,512]{4,3,2,1,0:T(8,128)} %bitcast.12) | data formatting | bytes 1048576

commit v4 on v3

--- a/solution.py
+++ b/solution.py
@@ -429,6 +429,17 @@
         send(dp_send.at[peers[d]], dp_recv.at[d], dp_sem, d, {"dp": peers[d]}).wait()
         total = total + dp_recv[d].astype(F32)
     weight_out[...] = total[:rows_dev]
+
+
+def hand_over(weight_in, tile_in, weight_out, tile_out, sems):
+    copies = [
+        pltpu.make_async_copy(tile_in, tile_out, sems.at[0]),
+        pltpu.make_async_copy(weight_in, weight_out, sems.at[1]),
+    ]
+    for copy in copies:
+        copy.start()
+    for copy in copies:
+        copy.wait()
 
 
 def per_device(
@@ -529,6 +540,17 @@
         zone_counts[:, :1],
         grad_out[0].reshape(rows, channels),
     )
+    if reduce_here:
+        weight_out, tile_out = pl.pallas_call(
+            hand_over,
+            out_shape=(
+                jax.ShapeDtypeStruct(weight_shape, F32),
+                jax.ShapeDtypeStruct((tiles * 16, inner), F32),
+            ),
+            in_specs=[hbm] * 2,
+            out_specs=(hbm, hbm),
+            scratch_shapes=[pltpu.SemaphoreType.DMA((2,))],
+        )(weight_out, tile_out)
     weight_grads = weight_out.reshape(-1)
     if not reduce_here:
         weight_grads = lax.psum_scatter(

time: 45.1 us -> 62.9 us (1.39)
  Pallas kernels: 39.7 us -> 61.1 us
  local copies, waits for them, and re-layouts: 3.46 us -> 0 us
    pallas_call x0 -> x1, Pallas kernels: none -> 21.3 us  [per_device(): pl.pallas_call(hand_over, out_shape=(jax.ShapeDtypeStruct(weight_shape, F...]
    unnamed x2 -> x0, local copies, waits for them, and re-layouts: 3.46 us -> none
where the time goes in v4:
time: 62.9 us; the launch traced here: 62.4 us
  Pallas kernels  61.1 us (97%)
  between operations  1.29 us (2%)
    pallas_call x1, Pallas kernels, per_device(): pl.pallas_call(functools.partial(kernel, cfg), out_shape=(jax.ShapeDtypeS...  39.7 us
    pallas_call x1, Pallas kernels, per_device(): pl.pallas_call(hand_over, out_shape=(jax.ShapeDtypeStruct(weight_shape, F...  21.3 us

profile of v4, /device:TPU:0, one launch (start us, length us, event | category | flops | bytes accessed | tf_op | source)
XLA Modules:
  0.0 62.4 jit_solution(5620773889830611860)
XLA Ops:
  1.3 39.7 %shard_map.113 = (f32[280,128]{1,0:T(8,128)}, f32[256,512]{1,0:T(8,128)}) custom-call(bf16[16,256,128]{2,1,0:T(8,128)(2,1)} %bitcast.10, bf16[576,256]{1,0:T(8,128)(2,1)} %constant.2.clone.selector_hbm, bf16[3,1152,128]{2,1,0:T(8,128)(2,1)} %bitcast.11, bf16[128,512]{1,0:T(8,128)(2,1)} %query_w_hbm.1, bf16[512,128]{1,0:T(8,128)(2,1)} %out_w_hbm.1, ...), custom_call_target="tpu_custom_call" | custom-call | tf_op jit(solution)/shard_map/pallas_call | solution.py:477
  41.0 21.3 %shard_map.114 = (f32[280,128]{1,0:T(8,128)}, f32[256,512]{1,0:T(8,128)}) custom-call(f32[280,128]{1,0:T(8,128)} %get-tuple-element.6.weight_in, f32[256,512]{1,0:T(8,128)} %get-tuple-element.7.tile_in), custom_call_target="tpu_custom_call" | custom-call | tf_op jit(solution)/shard_map/pallas_call | solution.py:544
